TPU v7x, 32 devices: a whole 2x2x4 slice. The times are simulated.
32 devices in a mesh: grp: 2 (over y), src: 4 (over z), tile: 4 (over x, core).
Axes of the slice: x: 2, y: 2, z: 4, core: 2. Of those that a mesh axis runs over, the one named last changes fastest.
Arguments:
- mask: bfloat16 [4096, 2048], P(('grp', 'tile')), parts along dimension 0, may hold values from -1 to 1
- cotangent: bfloat16 [4096, 2048], P(('grp', 'tile')), parts along dimension 0, may hold values from -6 to 6
- pupil_phase: float32 [64, 64], replicated, may hold values from -3.140625 to 3.140625
- source_weight: float32 [12288], replicated, may hold values from 0.2 to 1
- shift_table: int32 [12288, 2], replicated, may hold values from 0 to 64
- source_ids: int32 [8, 8], P(('grp', 'src')), parts along dimension 0, may hold values from 0 to 12287
- source_count: int32 [8], P(('grp', 'src')), parts along dimension 0, may hold values from 1 to 8, as said below
Outputs:
- grad_mask: float32 [8, 512, 2048], P(('grp', 'tile'), 'src'), parts along dimension 0
There are 2 independent parts, one for each index of `grp`. A program takes and returns all parts, laid end to end along the dimension named above; an argument that names none is the same for every part. Nothing has to cross between parts.
Inputs may be any that keep to these rules, and one draw needn't show every extreme that they name: `source_count`: every src index has at least one used slot, and in every draw some src index uses all 8 slots.
All inputs are finite; a program needn't handle non-finite values.
Results may differ from a plain program's by a relative error of at most 0.008.
Values sent between devices are 32-bit elements; how exact they have to be, the bound alone decides.
No kernel may reach another device: no remote copies, remote signals or barrier semaphores. Data moves between devices by JAX's collectives and lax.ppermute only.
A program may use at most 64 MiB of HBM per device.

v0:
```python
import math

import jax
import jax.numpy as jnp
from jax import lax
from jax.sharding import PartitionSpec as P

COLS = 2048
TILE_ROWS = 2048
BAND = 128
PUPIL = 64
SLOTS = 8


def angles(positions, freqs, length):
    product = positions[:, None] * freqs[None, :] % length
    return product.astype(jnp.float32) * (2.0 * math.pi / length)


def centered(count):
    return jnp.arange(count, dtype=jnp.int32) - count // 2


def contract_rows(left, right):
    return lax.dot_general(
        left,
        right,
        (((0,), (0,)), ((), ())),
        precision=lax.Precision.HIGHEST,
        preferred_element_type=jnp.float32,
    )


def body(mask, cotangent, pupil_phase, source_weight, shift_table, source_ids, source_count):
    height = mask.shape[0]
    columns = mask.shape[1]
    scale = 1.0 / math.sqrt(TILE_ROWS * COLS)
    tile_start = lax.axis_index("tile") * height
    row_positions = tile_start + jnp.arange(height, dtype=jnp.int32)
    col_positions = jnp.arange(columns, dtype=jnp.int32)
    column_angle = angles(col_positions, centered(BAND), columns)
    column_cos = jnp.cos(column_angle)
    column_sin = jnp.sin(column_angle)
    forward_cols = jnp.concatenate([column_cos, -column_sin], 1).astype(jnp.bfloat16)
    row_angle = angles(row_positions, centered(BAND), TILE_ROWS)
    forward_rows = jnp.concatenate([jnp.cos(row_angle), jnp.sin(row_angle)], 1).astype(jnp.bfloat16)
    column_part = jnp.dot(mask, forward_cols, preferred_element_type=jnp.float32).astype(
        jnp.bfloat16
    )
    blocks = lax.dot_general(
        forward_rows, column_part, (((0,), (0,)), ((), ())), preferred_element_type=jnp.float32
    )
    partial_spec = jnp.stack(
        [blocks[:BAND, :BAND] + blocks[BAND:, BAND:], blocks[:BAND, BAND:] - blocks[BAND:, :BAND]]
    )
    spectrum_sum = lax.psum(partial_spec, "tile")
    spectrum = (spectrum_sum * scale).astype(jnp.bfloat16)
    grid_u = jnp.arange(PUPIL, dtype=jnp.int32)
    radius = (2 * grid_u[:, None] - PUPIL + 1) ** 2 + (2 * grid_u[None, :] - PUPIL + 1) ** 2
    inside = radius <= PUPIL * PUPIL
    pupil_real = jnp.where(inside, jnp.cos(pupil_phase), 0.0)
    pupil_imag = jnp.where(inside, jnp.sin(pupil_phase), 0.0)
    pupil_angle = angles(col_positions, centered(PUPIL), columns)
    pupil_cols = jnp.concatenate([jnp.cos(pupil_angle).T, jnp.sin(pupil_angle).T], 0).astype(
        jnp.bfloat16
    )
    image_angle = angles(row_positions, centered(PUPIL), TILE_ROWS)
    image_cos = jnp.cos(image_angle)
    image_sin = jnp.sin(image_angle)
    image_rows = jnp.concatenate(
        [jnp.concatenate([image_cos, -image_sin], 1), jnp.concatenate([image_sin, image_cos], 1)], 0
    ).astype(jnp.bfloat16)

    def contribution(source, totals):
        offset_x = shift_table[source, 0]
        offset_y = shift_table[source, 1]
        start = (jnp.int32(0), offset_y, offset_x)
        window = lax.dynamic_slice(spectrum, start, (2, PUPIL, PUPIL)).astype(jnp.float32)
        amp_real = pupil_real * window[0] - pupil_imag * window[1]
        amp_imag = pupil_real * window[1] + pupil_imag * window[0]
        amplitude = jnp.concatenate(
            [jnp.concatenate([amp_real, -amp_imag], 1), jnp.concatenate([amp_imag, amp_real], 1)], 0
        ).astype(jnp.bfloat16)
        halfway = jnp.dot(amplitude, pupil_cols, preferred_element_type=jnp.float32).astype(
            jnp.bfloat16
        )
        field = jnp.dot(image_rows, halfway, preferred_element_type=jnp.float32) * (1.0 / PUPIL)
        factor = 2.0 / SLOTS * source_weight[source]
        field_grad = (
            (field.reshape(2, height, columns) * factor * cotangent[None])
            .astype(jnp.bfloat16)
            .reshape(2 * height, columns)
        )
        back = lax.dot_general(
            field_grad, pupil_cols, (((1,), (1,)), ((), ())), preferred_element_type=jnp.float32
        )
        back_real = back[:height, :PUPIL] + back[height:, PUPIL:]
        back_imag = back[height:, :PUPIL] - back[:height, PUPIL:]
        grad_real = (
            contract_rows(image_cos, back_real) + contract_rows(image_sin, back_imag)
        ) / PUPIL
        grad_imag = (
            contract_rows(image_cos, back_imag) - contract_rows(image_sin, back_real)
        ) / PUPIL
        spec_real = pupil_real * grad_real + pupil_imag * grad_imag
        spec_imag = pupil_real * grad_imag - pupil_imag * grad_real
        current = lax.dynamic_slice(totals, start, (2, PUPIL, PUPIL))
        return lax.dynamic_update_slice(totals, current + jnp.stack([spec_real, spec_imag]), start)

    empty = jnp.zeros((2, BAND, BAND), jnp.float32)

    def own_slot(step, totals):
        return contribution(source_ids[0, step], totals)

    band_grad = lax.fori_loop(jnp.int32(0), source_count[0], own_slot, empty)
    back_cols = jnp.concatenate([column_cos, column_sin], 1)
    portion = height // lax.axis_size("src")
    tile_grad = lax.psum(band_grad, "tile")
    left_side = jnp.concatenate(
        [
            jnp.concatenate([tile_grad[0], -tile_grad[1]], 1),
            jnp.concatenate([tile_grad[1], tile_grad[0]], 1),
        ],
        0,
    )
    positions = tile_start + jnp.arange(portion * lax.axis_size("src"), dtype=jnp.int32)
    local_angle = angles(positions, centered(BAND), TILE_ROWS)
    row_side = jnp.concatenate([jnp.cos(local_angle), -jnp.sin(local_angle)], 1)
    mixed = jnp.dot(
        row_side, left_side, precision=lax.Precision.HIGHEST, preferred_element_type=jnp.float32
    )
    result = lax.psum_scatter(
        lax.dot_general(
            mixed,
            back_cols,
            (((1,), (1,)), ((), ())),
            precision=lax.Precision.HIGHEST,
            preferred_element_type=jnp.float32,
        )
        * scale,
        "src",
        scatter_dimension=0,
        tiled=True,
    )
    return result.reshape(1, portion, columns)


def solution(mesh):
    placed = (
        P(("grp", "tile"), None),
        P(("grp", "tile"), None),
        P(),
        P(),
        P(),
        P(("grp", "src"), None),
        P(("grp", "src")),
    )
    return jax.shard_map(
        body, mesh=mesh, in_specs=placed, out_specs=P(("grp", "tile"), "src", None), check_vma=False
    )
```

profile of v0, /device:TPU:0, one launch (start us, length us, event | category | flops | bytes accessed | tf_op | source)
XLA Modules:
  0.0 520.2 jit_solution(4114600384989557708)
XLA Ops:
  6.5 5.6 %fusion.71 = (f32[2048,128]{1,0:T(8,128)}, bf16[2048,128]{1,0:T(8,128)(2,1)S(1)}, bf16[2048,128]{1,0:T(8,128)(2,1)S(1)}, f32[2048,128]{1,0:T(8,128)}) fusion(s32[128]{0:T(128)S(1)} %iota_add_fusion.2), kind=kLoop, calls=%fused_computation.97 | loop fusion | flops 4456448 | bytes 3146240 | tf_op jit(solution)/shard_map/cos | solution.py:42
  23.3 27.6 %all-reduce.3.cloned.1.call-done = f32[2,128,128]{2,1,0:T(8,128)} async-done(((f32[2,128,128]{2,1,0:T(8,128)}), f32[2,128,128]{2,1,0:T(8,128)}) %all-reduce.3.cloned.1.call-update) | async-done | bytes 131088 | tf_op jit(solution)/shard_map/psum | solution.py:56
  52.5 343.6 %while.14 = (s32[]{:T(128)}, f32[2,128,128]{1,2,0:T(8,128)S(1)}, s32[]{:T(128)}, s32[1,8]{1,0:T(1,128)S(1)}, s32[12288,2]{0,1:T(2,128)}, /*index=5*/bf16[2,128,1...) while((s32[]{:T(128)}, f32[2,128,128]{1,2,0:T(8,128)S(1)}, ...), condition=%wide.region_2.3_spmd.clone.clone, body=%wide.region_1.2_spmd.clone.clone.sunk | while | flops 1250271232 | bytes 48834044 | solution.py:115
  57.5 4.7 mul.915
  62.3 5.3 %copy.18 = f32[256,8,2,512]{3,1,2,0:T(8,128)} copy(f32[256,8,2,512]{3,2,1,0:T(2,128)S(1)} %bitcast.85) | data formatting | bytes 16777216 | tf_op jit(solution)/shard_map/while
  78.7 6.1 %fusion.134 = f32[1024,128]{0,1:T(8,128)} fusion(bf16[128,2048]{1,0:T(8,128)(2,1)S(1)} %get-tuple-element.477, f32[1024,2048]{0,1:T(8,128)} %bitcast.84, bf16[128,2048]{1,0:T(8,128)(2,1)S(1)} %convolution_convert_fusion.3, bf16[1024,128]{1,0:T(8,128)(2,1)S(1)} %get-tuple-element.478, f32[]{:T(128)} %bitcast.83), kind=kOutput, calls=%fused_computation.5.clone.1 | convolution fusion | flops 1080033280 | bytes 10223620 | tf_op jit(solution)/shard_map/while/body/dot_general | solution.py:94
  100.4 4.7 mul.915
  105.2 5.3 %copy.18 = f32[256,8,2,512]{3,1,2,0:T(8,128)} copy(f32[256,8,2,512]{3,2,1,0:T(2,128)S(1)} %bitcast.85) | data formatting | bytes 16777216 | tf_op jit(solution)/shard_map/while
  121.6 6.1 %fusion.134 = f32[1024,128]{0,1:T(8,128)} fusion(bf16[128,2048]{1,0:T(8,128)(2,1)S(1)} %get-tuple-element.477, f32[1024,2048]{0,1:T(8,128)} %bitcast.84, bf16[128,2048]{1,0:T(8,128)(2,1)S(1)} %convolution_convert_fusion.3, bf16[1024,128]{1,0:T(8,128)(2,1)S(1)} %get-tuple-element.478, f32[]{:T(128)} %bitcast.83), kind=kOutput, calls=%fused_computation.5.clone.1 | convolution fusion | flops 1080033280 | bytes 10223620 | tf_op jit(solution)/shard_map/while/body/dot_general | solution.py:94
  143.2 4.7 mul.915
  148.0 5.3 %copy.18 = f32[256,8,2,512]{3,1,2,0:T(8,128)} copy(f32[256,8,2,512]{3,2,1,0:T(2,128)S(1)} %bitcast.85) | data formatting | bytes 16777216 | tf_op jit(solution)/shard_map/while
  164.4 6.1 %fusion.134 = f32[1024,128]{0,1:T(8,128)} fusion(bf16[128,2048]{1,0:T(8,128)(2,1)S(1)} %get-tuple-element.477, f32[1024,2048]{0,1:T(8,128)} %bitcast.84, bf16[128,2048]{1,0:T(8,128)(2,1)S(1)} %convolution_convert_fusion.3, bf16[1024,128]{1,0:T(8,128)(2,1)S(1)} %get-tuple-element.478, f32[]{:T(128)} %bitcast.83), kind=kOutput, calls=%fused_computation.5.clone.1 | convolution fusion | flops 1080033280 | bytes 10223620 | tf_op jit(solution)/shard_map/while/body/dot_general | solution.py:94
  181.9 4.2 copy.17
  186.1 4.7 mul.915
  190.8 5.3 %copy.18 = f32[256,8,2,512]{3,1,2,0:T(8,128)} copy(f32[256,8,2,512]{3,2,1,0:T(2,128)S(1)} %bitcast.85) | data formatting | bytes 16777216 | tf_op jit(solution)/shard_map/while
  207.3 6.1 %fusion.134 = f32[1024,128]{0,1:T(8,128)} fusion(bf16[128,2048]{1,0:T(8,128)(2,1)S(1)} %get-tuple-element.477, f32[1024,2048]{0,1:T(8,128)} %bitcast.84, bf16[128,2048]{1,0:T(8,128)(2,1)S(1)} %convolution_convert_fusion.3, bf16[1024,128]{1,0:T(8,128)(2,1)S(1)} %get-tuple-element.478, f32[]{:T(128)} %bitcast.83), kind=kOutput, calls=%fused_computation.5.clone.1 | convolution fusion | flops 1080033280 | bytes 10223620 | tf_op jit(solution)/shard_map/while/body/dot_general | solution.py:94
  224.8 4.2 copy.17
  229.0 4.7 mul.915
  233.7 5.3 %copy.18 = f32[256,8,2,512]{3,1,2,0:T(8,128)} copy(f32[256,8,2,512]{3,2,1,0:T(2,128)S(1)} %bitcast.85) | data formatting | bytes 16777216 | tf_op jit(solution)/shard_map/while
  250.2 6.1 %fusion.134 = f32[1024,128]{0,1:T(8,128)} fusion(bf16[128,2048]{1,0:T(8,128)(2,1)S(1)} %get-tuple-element.477, f32[1024,2048]{0,1:T(8,128)} %bitcast.84, bf16[128,2048]{1,0:T(8,128)(2,1)S(1)} %convolution_convert_fusion.3, bf16[1024,128]{1,0:T(8,128)(2,1)S(1)} %get-tuple-element.478, f32[]{:T(128)} %bitcast.83), kind=kOutput, calls=%fused_computation.5.clone.1 | convolution fusion | flops 1080033280 | bytes 10223620 | tf_op jit(solution)/shard_map/while/body/dot_general | solution.py:94
  271.8 4.7 mul.915
  276.6 5.3 %copy.18 = f32[256,8,2,512]{3,1,2,0:T(8,128)} copy(f32[256,8,2,512]{3,2,1,0:T(2,128)S(1)} %bitcast.85) | data formatting | bytes 16777216 | tf_op jit(solution)/shard_map/while
  293.0 6.1 %fusion.134 = f32[1024,128]{0,1:T(8,128)} fusion(bf16[128,2048]{1,0:T(8,128)(2,1)S(1)} %get-tuple-element.477, f32[1024,2048]{0,1:T(8,128)} %bitcast.84, bf16[128,2048]{1,0:T(8,128)(2,1)S(1)} %convolution_convert_fusion.3, bf16[1024,128]{1,0:T(8,128)(2,1)S(1)} %get-tuple-element.478, f32[]{:T(128)} %bitcast.83), kind=kOutput, calls=%fused_computation.5.clone.1 | convolution fusion | flops 1080033280 | bytes 10223620 | tf_op jit(solution)/shard_map/while/body/dot_general | solution.py:94
  314.7 4.7 mul.915
  319.4 5.3 %copy.18 = f32[256,8,2,512]{3,1,2,0:T(8,128)} copy(f32[256,8,2,512]{3,2,1,0:T(2,128)S(1)} %bitcast.85) | data formatting | bytes 16777216 | tf_op jit(solution)/shard_map/while
  335.8 6.1 %fusion.134 = f32[1024,128]{0,1:T(8,128)} fusion(bf16[128,2048]{1,0:T(8,128)(2,1)S(1)} %get-tuple-element.477, f32[1024,2048]{0,1:T(8,128)} %bitcast.84, bf16[128,2048]{1,0:T(8,128)(2,1)S(1)} %convolution_convert_fusion.3, bf16[1024,128]{1,0:T(8,128)(2,1)S(1)} %get-tuple-element.478, f32[]{:T(128)} %bitcast.83), kind=kOutput, calls=%fused_computation.5.clone.1 | convolution fusion | flops 1080033280 | bytes 10223620 | tf_op jit(solution)/shard_map/while/body/dot_general | solution.py:94
  357.5 4.7 mul.915
  362.2 5.3 %copy.18 = f32[256,8,2,512]{3,1,2,0:T(8,128)} copy(f32[256,8,2,512]{3,2,1,0:T(2,128)S(1)} %bitcast.85) | data formatting | bytes 16777216 | tf_op jit(solution)/shard_map/while
  378.7 6.1 %fusion.134 = f32[1024,128]{0,1:T(8,128)} fusion(bf16[128,2048]{1,0:T(8,128)(2,1)S(1)} %get-tuple-element.477, f32[1024,2048]{0,1:T(8,128)} %bitcast.84, bf16[128,2048]{1,0:T(8,128)(2,1)S(1)} %convolution_convert_fusion.3, bf16[1024,128]{1,0:T(8,128)(2,1)S(1)} %get-tuple-element.478, f32[]{:T(128)} %bitcast.83), kind=kOutput, calls=%fused_computation.5.clone.1 | convolution fusion | flops 1080033280 | bytes 10223620 | tf_op jit(solution)/shard_map/while/body/dot_general | solution.py:94
  397.1 29.5 %all-reduce.5.cloned.1.call-done = f32[2,128,128]{1,2,0:T(8,128)} async-done(((f32[2,128,128]{1,2,0:T(8,128)}), f32[2,128,128]{1,2,0:T(8,128)}) %all-reduce.5.cloned.1.call-update) | async-done | bytes 131088 | tf_op jit(solution)/shard_map/psum | solution.py:118
  429.9 6.7 %convolution_multiply_fusion = f32[512,2048]{1,0:T(8,128)} fusion(f32[512,256]{1,0:T(8,128)S(1)} %fusion.64, f32[2048,128]{1,0:T(8,128)} %get-tuple-element.323, f32[2048,128]{1,0:T(8,128)} %get-tuple-element.320), kind=kOutput, calls=%fused_computation.62 | convolution fusion | flops 3222798336 | bytes 6815744 | tf_op jit(solution)/shard_map/dot_general | solution.py:133
  436.7 76.9 %reduce-scatter.2.cloned.1.call-done = f32[128,2048]{1,0:T(8,128)} async-done(((f32[512,2048]{1,0:T(8,128)}), f32[128,2048]{1,0:T(8,128)}) %reduce-scatter.2.cloned.1.call-update) | async-done | bytes 1048592 | tf_op jit(solution)/shard_map/reduce_scatter | solution.py:132
  (213 shorter events, 165.1 us)
Async XLA Ops:
  6.5 44.4 %all-reduce.3.cloned.1.call-start = ((), (), s32[]{:S(2)}) async-start(), calls=%async_computation.1 | async-start | bytes 262144 | tf_op jit(solution)/shard_map/psum | solution.py:56
  14.1 38.4 %copy-start.6 = (s32[1,8]{1,0:T(1,128)S(1)}, s32[1,8]{1,0:T(1,128)}, u32[]{:S(2)}) copy-start(s32[1,8]{1,0:T(1,128)} %param.14) | copy-start | bytes 100
  16.7 409.9 %all-reduce.5.cloned.1.call-start = ((), (), s32[]{:S(2)}) async-start(), calls=%async_computation.2 | async-start | bytes 262144 | tf_op jit(solution)/shard_map/psum | solution.py:118
  53.3 23.0 %copy-start.2 = (f32[64,64]{0,1:T(8,128)}, f32[64,64]{0,1:T(8,128)S(1)}, u32[]{:S(2)}) copy-start(f32[64,64]{0,1:T(8,128)S(1)} %get-tuple-element.476) | copy-start | bytes 49156 | tf_op jit(solution)/shard_map/while
  53.3 23.0 %copy-start.4 = (f32[64,64]{0,1:T(8,128)}, f32[64,64]{0,1:T(8,128)S(1)}, u32[]{:S(2)}) copy-start(f32[64,64]{0,1:T(8,128)S(1)} %get-tuple-element.475) | copy-start | bytes 49156 | tf_op jit(solution)/shard_map/while
  84.8 10.8 %copy-start.3 = (f32[64,64]{0,1:T(8,128)S(1)}, f32[64,64]{0,1:T(8,128)}, u32[]{:S(2)}) copy-start(f32[64,64]{0,1:T(8,128)} %copy-done.2) | copy-start | bytes 49156 | tf_op jit(solution)/shard_map/while
  84.8 10.8 %copy-start.5 = (f32[64,64]{0,1:T(8,128)S(1)}, f32[64,64]{0,1:T(8,128)}, u32[]{:S(2)}) copy-start(f32[64,64]{0,1:T(8,128)} %copy-done.4) | copy-start | bytes 49156 | tf_op jit(solution)/shard_map/while
  96.2 23.0 %copy-start.2 = (f32[64,64]{0,1:T(8,128)}, f32[64,64]{0,1:T(8,128)S(1)}, u32[]{:S(2)}) copy-start(f32[64,64]{0,1:T(8,128)S(1)} %get-tuple-element.476) | copy-start | bytes 49156 | tf_op jit(solution)/shard_map/while
  96.2 23.0 %copy-start.4 = (f32[64,64]{0,1:T(8,128)}, f32[64,64]{0,1:T(8,128)S(1)}, u32[]{:S(2)}) copy-start(f32[64,64]{0,1:T(8,128)S(1)} %get-tuple-element.475) | copy-start | bytes 49156 | tf_op jit(solution)/shard_map/while
  139.0 23.0 %copy-start.2 = (f32[64,64]{0,1:T(8,128)}, f32[64,64]{0,1:T(8,128)S(1)}, u32[]{:S(2)}) copy-start(f32[64,64]{0,1:T(8,128)S(1)} %get-tuple-element.476) | copy-start | bytes 49156 | tf_op jit(solution)/shard_map/while
  139.1 23.0 %copy-start.4 = (f32[64,64]{0,1:T(8,128)}, f32[64,64]{0,1:T(8,128)S(1)}, u32[]{:S(2)}) copy-start(f32[64,64]{0,1:T(8,128)S(1)} %get-tuple-element.475) | copy-start | bytes 49156 | tf_op jit(solution)/shard_map/while
  170.5 10.7 %copy-start.3 = (f32[64,64]{0,1:T(8,128)S(1)}, f32[64,64]{0,1:T(8,128)}, u32[]{:S(2)}) copy-start(f32[64,64]{0,1:T(8,128)} %copy-done.2) | copy-start | bytes 49156 | tf_op jit(solution)/shard_map/while
  170.5 10.7 %copy-start.5 = (f32[64,64]{0,1:T(8,128)S(1)}, f32[64,64]{0,1:T(8,128)}, u32[]{:S(2)}) copy-start(f32[64,64]{0,1:T(8,128)} %copy-done.4) | copy-start | bytes 49156 | tf_op jit(solution)/shard_map/while
  181.9 23.0 %copy-start.2 = (f32[64,64]{0,1:T(8,128)}, f32[64,64]{0,1:T(8,128)S(1)}, u32[]{:S(2)}) copy-start(f32[64,64]{0,1:T(8,128)S(1)} %get-tuple-element.476) | copy-start | bytes 49156 | tf_op jit(solution)/shard_map/while
  181.9 23.0 %copy-start.4 = (f32[64,64]{0,1:T(8,128)}, f32[64,64]{0,1:T(8,128)S(1)}, u32[]{:S(2)}) copy-start(f32[64,64]{0,1:T(8,128)S(1)} %get-tuple-element.475) | copy-start | bytes 49156 | tf_op jit(solution)/shard_map/while
  213.4 10.8 %copy-start.3 = (f32[64,64]{0,1:T(8,128)S(1)}, f32[64,64]{0,1:T(8,128)}, u32[]{:S(2)}) copy-start(f32[64,64]{0,1:T(8,128)} %copy-done.2) | copy-start | bytes 49156 | tf_op jit(solution)/shard_map/while
  213.4 10.8 %copy-start.5 = (f32[64,64]{0,1:T(8,128)S(1)}, f32[64,64]{0,1:T(8,128)}, u32[]{:S(2)}) copy-start(f32[64,64]{0,1:T(8,128)} %copy-done.4) | copy-start | bytes 49156 | tf_op jit(solution)/shard_map/while
  224.8 23.0 %copy-start.2 = (f32[64,64]{0,1:T(8,128)}, f32[64,64]{0,1:T(8,128)S(1)}, u32[]{:S(2)}) copy-start(f32[64,64]{0,1:T(8,128)S(1)} %get-tuple-element.476) | copy-start | bytes 49156 | tf_op jit(solution)/shard_map/while
  224.8 23.0 %copy-start.4 = (f32[64,64]{0,1:T(8,128)}, f32[64,64]{0,1:T(8,128)S(1)}, u32[]{:S(2)}) copy-start(f32[64,64]{0,1:T(8,128)S(1)} %get-tuple-element.475) | copy-start | bytes 49156 | tf_op jit(solution)/shard_map/while
  256.2 10.7 %copy-start.3 = (f32[64,64]{0,1:T(8,128)S(1)}, f32[64,64]{0,1:T(8,128)}, u32[]{:S(2)}) copy-start(f32[64,64]{0,1:T(8,128)} %copy-done.2) | copy-start | bytes 49156 | tf_op jit(solution)/shard_map/while
  256.2 10.7 %copy-start.5 = (f32[64,64]{0,1:T(8,128)S(1)}, f32[64,64]{0,1:T(8,128)}, u32[]{:S(2)}) copy-start(f32[64,64]{0,1:T(8,128)} %copy-done.4) | copy-start | bytes 49156 | tf_op jit(solution)/shard_map/while
  267.6 23.0 %copy-start.2 = (f32[64,64]{0,1:T(8,128)}, f32[64,64]{0,1:T(8,128)S(1)}, u32[]{:S(2)}) copy-start(f32[64,64]{0,1:T(8,128)S(1)} %get-tuple-element.476) | copy-start | bytes 49156 | tf_op jit(solution)/shard_map/while
  267.6 23.0 %copy-start.4 = (f32[64,64]{0,1:T(8,128)}, f32[64,64]{0,1:T(8,128)S(1)}, u32[]{:S(2)}) copy-start(f32[64,64]{0,1:T(8,128)S(1)} %get-tuple-element.475) | copy-start | bytes 49156 | tf_op jit(solution)/shard_map/while
  299.1 10.7 %copy-start.3 = (f32[64,64]{0,1:T(8,128)S(1)}, f32[64,64]{0,1:T(8,128)}, u32[]{:S(2)}) copy-start(f32[64,64]{0,1:T(8,128)} %copy-done.2) | copy-start | bytes 49156 | tf_op jit(solution)/shard_map/while
  299.1 10.7 %copy-start.5 = (f32[64,64]{0,1:T(8,128)S(1)}, f32[64,64]{0,1:T(8,128)}, u32[]{:S(2)}) copy-start(f32[64,64]{0,1:T(8,128)} %copy-done.4) | copy-start | bytes 49156 | tf_op jit(solution)/shard_map/while
  310.5 23.0 %copy-start.2 = (f32[64,64]{0,1:T(8,128)}, f32[64,64]{0,1:T(8,128)S(1)}, u32[]{:S(2)}) copy-start(f32[64,64]{0,1:T(8,128)S(1)} %get-tuple-element.476) | copy-start | bytes 49156 | tf_op jit(solution)/shard_map/while
  310.5 23.0 %copy-start.4 = (f32[64,64]{0,1:T(8,128)}, f32[64,64]{0,1:T(8,128)S(1)}, u32[]{:S(2)}) copy-start(f32[64,64]{0,1:T(8,128)S(1)} %get-tuple-element.475) | copy-start | bytes 49156 | tf_op jit(solution)/shard_map/while
  353.3 23.0 %copy-start.2 = (f32[64,64]{0,1:T(8,128)}, f32[64,64]{0,1:T(8,128)S(1)}, u32[]{:S(2)}) copy-start(f32[64,64]{0,1:T(8,128)S(1)} %get-tuple-element.476) | copy-start | bytes 49156 | tf_op jit(solution)/shard_map/while
  353.3 23.0 %copy-start.4 = (f32[64,64]{0,1:T(8,128)}, f32[64,64]{0,1:T(8,128)S(1)}, u32[]{:S(2)}) copy-start(f32[64,64]{0,1:T(8,128)S(1)} %get-tuple-element.475) | copy-start | bytes 49156 | tf_op jit(solution)/shard_map/while
  384.7 10.7 %copy-start.3 = (f32[64,64]{0,1:T(8,128)S(1)}, f32[64,64]{0,1:T(8,128)}, u32[]{:S(2)}) copy-start(f32[64,64]{0,1:T(8,128)} %copy-done.2) | copy-start | bytes 49156 | tf_op jit(solution)/shard_map/while
  384.7 10.7 %copy-start.5 = (f32[64,64]{0,1:T(8,128)S(1)}, f32[64,64]{0,1:T(8,128)}, u32[]{:S(2)}) copy-start(f32[64,64]{0,1:T(8,128)} %copy-done.4) | copy-start | bytes 49156 | tf_op jit(solution)/shard_map/while
  396.8 116.8 %reduce-scatter.2.cloned.1.call-start = ((), (), s32[]{:S(2)}) async-start(), calls=%async_computation.3 | async-start | bytes 5242880 | tf_op jit(solution)/shard_map/reduce_scatter | solution.py:132
  (6 other events, 51.0 us)
Sparse Core Ops, SparseCore 0:
  16.8 34.0 all-reduce.2
  396.9 29.5 all-reduce.4
  436.8 76.7 reduce-scatter.1
where the time goes:
time: 525 us; the launch traced here: 520 us
  local copies, waits for them, and re-layouts  162 us (31%)
  matrix products  135 us (26%)
  waiting for transfers between devices  134 us (26%)
  loops' own time  58.3 us (11%)
  other arithmetic  17.2 us (3%)
  between operations  13.2 us (3%)
    reduce_scatter x1, waiting for transfers between devices, body(): lax.psum_scatter(lax.dot_general(mixed, back_cols, (((1,), (1,)), ((), ()...  76.9 us
    dot_general x32, matrix products, contract_rows(): lax.dot_general(left, right, (((0,), (0,)), ((), ())), precision=lax.Prec...  73.4 us
    another operation x1, loops' own time, body(): band_grad = lax.fori_loop(jnp.int32(0), source_count[0], own_slot, empty)  58.3 us
    dot_general x8, matrix products, contribution(): lax.dot_general(field_grad, pupil_cols, (((1,), (1,)), ((), ())), preferr...  48.5 us
    while x72, local copies, waits for them, and re-layouts  42.7 us
    mul x8, local copies, waits for them, and re-layouts, contribution(): field.reshape(2, height, columns) * factor * cotangent[None]  37.9 us
    convert_element_type x8, local copies, waits for them, and re-layouts, contribution(): field.reshape(2, height, columns) * factor * cotangent[None]  33.4 us
    psum x1, waiting for transfers between devices, body(): tile_grad = lax.psum(band_grad, 'tile')  29.5 us
  transfers between devices with their start and end apart: 3, of which 3 were waited for; matrix products, arithmetic and copies ran while one was open for 1% of the time, Pallas kernels for 0%

commit v1 on v0

v1 whole, which is shorter than its diff:
```python
import functools
import math

import jax
import jax.numpy as jnp
import ml_dtypes
import numpy as np
from jax import lax
from jax.experimental import pallas as pl
from jax.experimental.pallas import tpu as pltpu
from jax.sharding import PartitionSpec as P

COLS = 2048
TILE_ROWS = 2048
BAND = 128
PUPIL = 64
SLOTS = 8
GRID = 128
CHUNKS = 4
GROUP = 4
OX, OY, WEIGHT, USED = range(4)

VMEM = pl.BlockSpec(memory_space=pltpu.VMEM)
SMEM = pl.BlockSpec(memory_space=pltpu.SMEM)
ANY = pl.BlockSpec(memory_space=pl.ANY)


def waves(positions, freqs, length):
    product = np.multiply.outer(positions, freqs) % length
    angle = product.astype(np.float64) * (2.0 * math.pi / length)
    return np.cos(angle), np.sin(angle)


def lowpass(positions, length):
    freqs = np.arange(1, PUPIL)
    step = length // GRID
    apart = np.arange(GRID)[None, :] * step - positions[:, None]
    product = (apart[:, :, None] * freqs) % length
    return (1.0 + 2.0 * np.cos(product * (2.0 * math.pi / length)).sum(2)) / GRID


def low(array):
    return np.ascontiguousarray(array).astype(ml_dtypes.bfloat16)


@functools.cache
def image_tables(columns, height, n_tile, n_src):
    band = np.arange(BAND) - BAND // 2
    cols = np.arange(columns)
    rows = np.arange(TILE_ROWS)
    cos, sin = waves(cols, band, columns)
    col_table = low(np.concatenate([cos, -sin, lowpass(cols, columns)], 1))
    cos, sin = waves(rows, band, TILE_ROWS)
    row_table = np.concatenate([cos, sin, lowpass(rows, TILE_ROWS)], 1)
    row_table = low(row_table.reshape(n_tile, height, 2 * BAND + GRID).transpose(0, 2, 1))
    portion = height // n_src
    out_table = np.concatenate([cos, -sin], 1).astype(np.float32)
    return col_table, row_table, out_table.reshape(n_tile * n_src, portion, 2 * BAND)


@functools.cache
def grid_tables():
    points = np.arange(GRID)
    cos, sin = waves(points, np.arange(BAND) - BAND // 2, GRID)
    cols_in = np.block([[cos.T, sin.T], [-sin.T, cos.T]])
    cols_out = np.block([[cos, -sin], [sin, cos]])
    cos, sin = waves(points, np.arange(PUPIL) - PUPIL // 2, GRID)
    rows_in = np.block([[cos, -sin], [sin, cos]])
    rows_out = np.block([[cos.T, sin.T], [-sin.T, cos.T]])
    return low(cols_in), low(rows_in), low(rows_out), low(cols_out)


def dot(left, right):
    return jnp.dot(left, right, preferred_element_type=jnp.float32)


def forward_kernel(
    ids, count, mask, cotangent, phase, weight, shift, col_table, row_table,
    partial, pupil, slots,
    mask_v, cot_v, col_v, row_v, shift_v, weight_v, sems,
):
    height, columns = mask.shape
    width = columns // CHUNKS
    tile = lax.axis_index("tile")
    chunk_copies = []
    for step in range(CHUNKS):
        part = pl.ds(step * width, width)
        copies = [
            pltpu.make_async_copy(col_table.at[part, :], col_v.at[part, :], sems.at[step, 0]),
            pltpu.make_async_copy(mask.at[:, part], mask_v.at[step], sems.at[step, 1]),
            pltpu.make_async_copy(cotangent.at[:, part], cot_v.at[step], sems.at[step, 2]),
        ]
        for copy in copies:
            copy.start()
        chunk_copies.append(copies)
    row_copy = pltpu.make_async_copy(row_table.at[tile], row_v, sems.at[CHUNKS, 0])
    row_copy.start()
    shift_copy = pltpu.make_async_copy(shift, shift_v, sems.at[CHUNKS, 1])
    shift_copy.start()
    weight_copy = pltpu.make_async_copy(weight, weight_v, sems.at[CHUNKS, 2])
    weight_copy.start()

    grid_u = lax.broadcasted_iota(jnp.int32, (PUPIL, PUPIL), 0)
    grid_v = lax.broadcasted_iota(jnp.int32, (PUPIL, PUPIL), 1)
    radius = (2 * grid_u - PUPIL + 1) ** 2 + (2 * grid_v - PUPIL + 1) ** 2
    inside = radius <= PUPIL * PUPIL
    rest = jnp.zeros((PUPIL, BAND - PUPIL), jnp.float32)
    pupil[:PUPIL, :] = jnp.concatenate([jnp.where(inside, jnp.cos(phase[...]), 0.0), rest], 1)
    pupil[PUPIL:, :] = jnp.concatenate([jnp.where(inside, jnp.sin(phase[...]), 0.0), rest], 1)

    for step in range(CHUNKS):
        for copy in chunk_copies[step]:
            copy.wait()
        part = pl.ds(step * width, width)
        mask_add = dot(mask_v[step], col_v[part, : 2 * BAND])
        cot_add = dot(cot_v[step], col_v[part, 2 * BAND :])
        mask_part = mask_add if step == 0 else mask_part + mask_add
        cot_part = cot_add if step == 0 else cot_part + cot_add

    row_copy.wait()
    blocks = dot(row_v[: 2 * BAND, :], mask_part.astype(jnp.bfloat16))
    partial[:BAND, :] = blocks[:BAND, :BAND] + blocks[BAND:, BAND:]
    partial[BAND : 2 * BAND, :] = blocks[:BAND, BAND:] - blocks[BAND:, :BAND]
    partial[2 * BAND :, :] = dot(row_v[2 * BAND :, :], cot_part.astype(jnp.bfloat16))

    shift_copy.wait()
    weight_copy.wait()
    lane = lax.broadcasted_iota(jnp.int32, (1, 128), 1)
    lines = []
    for slot in range(SLOTS):
        source = ids[0, slot]
        start = pl.multiple_of(source // 128 * 128, 128)
        here = lane == source % 128
        found = []
        for line in (shift_v[0:1, pl.ds(start, 128)], shift_v[1:2, pl.ds(start, 128)]):
            found.append(jnp.sum(jnp.where(here, line.astype(jnp.float32), 0.0), 1, keepdims=True))
        line = weight_v[pl.ds(source // 128, 1), :]
        found.append(jnp.sum(jnp.where(here, line, 0.0), 1, keepdims=True))
        used = jnp.where(slot < count[0], 1.0, 0.0)
        row = jnp.where(lane == OX, found[0], 0.0) + jnp.where(lane == OY, found[1], 0.0)
        row += jnp.where(lane == WEIGHT, found[2] * used, 0.0) + jnp.where(lane == USED, used, 0.0)
        lines.append(row)
    slots[...] = jnp.concatenate(lines, 0)


def forward(ids, count, mask, cotangent, phase, weight, shift, col_table, row_table):
    height, columns = mask.shape
    width = columns // CHUNKS
    lines = 2 * BAND + GRID
    return pl.pallas_call(
        forward_kernel,
        out_shape=(
            jax.ShapeDtypeStruct((lines, BAND), jnp.float32),
            jax.ShapeDtypeStruct((2 * PUPIL, BAND), jnp.float32),
            jax.ShapeDtypeStruct((SLOTS, 128), jnp.float32),
        ),
        in_specs=[SMEM, SMEM, ANY, ANY, VMEM, ANY, ANY, ANY, ANY],
        out_specs=(VMEM, VMEM, VMEM),
        scratch_shapes=[
            pltpu.VMEM((CHUNKS, height, width), jnp.bfloat16),
            pltpu.VMEM((CHUNKS, height, width), jnp.bfloat16),
            pltpu.VMEM(col_table.shape, jnp.bfloat16),
            pltpu.VMEM(row_table.shape[1:], jnp.bfloat16),
            pltpu.VMEM(shift.shape, jnp.int32),
            pltpu.VMEM(weight.shape, jnp.float32),
            pltpu.SemaphoreType.DMA((CHUNKS + 1, 3)),
        ],
        compiler_params=pltpu.CompilerParams(vmem_limit_bytes=32 * 1024 * 1024),
        cost_estimate=pl.CostEstimate(
            flops=2 * height * columns * lines, bytes_accessed=6 * 1024 * 1024, transcendentals=0
        ),
        name="forward",
    )(ids, count, mask, cotangent, phase, weight, shift, col_table, row_table)


def adjoint_kernel(n_src, n_tile, *refs):
    own, other = refs[:2]
    infos = refs[2 : 2 + n_src]
    (
        pupil, cols_in, rows_in, rows_out, cols_out, col_table, out_table,
        result,
        spec, image, band, col_v, out_v, list_x, list_y, list_w, sems,
    ) = refs[2 + n_src :]
    place = lax.axis_index("tile") * n_src + lax.axis_index("src")
    col_copy = pltpu.make_async_copy(col_table.at[:, pl.ds(0, 2 * BAND)], col_v, sems.at[0])
    col_copy.start()
    out_copy = pltpu.make_async_copy(out_table.at[place], out_v, sems.at[1])
    out_copy.start()

    scale = 1.0 / math.sqrt(TILE_ROWS * COLS)
    whole = own[...] + other[...]
    spec[...] = (whole[: 2 * BAND] * scale).astype(jnp.bfloat16).astype(jnp.float32)
    image[:GRID, :] = whole[2 * BAND :]
    image[GRID:, :] = whole[2 * BAND :]
    band[...] = jnp.zeros_like(band)

    total = jnp.int32(0)
    for info in infos:
        for slot in range(SLOTS):
            list_x[total] = info[slot, OX].astype(jnp.int32)
            list_y[total] = info[slot, OY].astype(jnp.int32)
            list_w[total] = info[slot, WEIGHT] * (2.0 / SLOTS / PUPIL / PUPIL)
            total = total + info[slot, USED].astype(jnp.int32)
    for slot in range(GROUP):
        list_x[total + slot] = jnp.int32(0)
        list_y[total + slot] = jnp.int32(0)
        list_w[total + slot] = jnp.float32(0.0)

    def group(step, carry):
        offsets, pupils, amplitudes = [], [], []
        for slot in range(GROUP):
            index = step * GROUP + slot
            offset_x, offset_y = list_x[index], list_y[index]
            real = pltpu.roll(pupil[:PUPIL, :], offset_x, 1)
            imag = pltpu.roll(pupil[PUPIL:, :], offset_x, 1)
            spec_real = spec[pl.ds(offset_y, PUPIL), :]
            spec_imag = spec[pl.ds(BAND + offset_y, PUPIL), :]
            amp_real = real * spec_real - imag * spec_imag
            amp_imag = real * spec_imag + imag * spec_real
            offsets.append(offset_y)
            pupils.append((real, imag, list_w[index]))
            amplitudes.append(jnp.concatenate([amp_real, amp_imag], 1).astype(jnp.bfloat16))
        halfway = dot(jnp.concatenate(amplitudes, 0), cols_in[...]).astype(jnp.bfloat16)
        halfway = jnp.concatenate(
            [
                jnp.concatenate(
                    [
                        halfway[slot * PUPIL : (slot + 1) * PUPIL, :GRID],
                        halfway[slot * PUPIL : (slot + 1) * PUPIL, GRID:],
                    ],
                    0,
                )
                for slot in range(GROUP)
            ],
            1,
        )
        field = dot(rows_in[...], halfway)
        field_grad = jnp.concatenate(
            [
                (field[:, slot * GRID : (slot + 1) * GRID] * image[...]).astype(jnp.bfloat16)
                for slot in range(GROUP)
            ],
            1,
        )
        back = dot(rows_out[...], field_grad).astype(jnp.bfloat16)
        back = jnp.concatenate(
            [
                jnp.concatenate(
                    [
                        back[:PUPIL, slot * GRID : (slot + 1) * GRID],
                        back[PUPIL:, slot * GRID : (slot + 1) * GRID],
                    ],
                    1,
                )
                for slot in range(GROUP)
            ],
            0,
        )
        grad = dot(back, cols_out[...])
        for slot in range(GROUP):
            real, imag, factor = pupils[slot]
            grad_real = grad[slot * PUPIL : (slot + 1) * PUPIL, :BAND] * factor
            grad_imag = grad[slot * PUPIL : (slot + 1) * PUPIL, BAND:] * factor
            rows = pl.ds(offsets[slot], PUPIL)
            band[rows, :] = band[rows, :] + (real * grad_real + imag * grad_imag)
            rows = pl.ds(BAND + offsets[slot], PUPIL)
            band[rows, :] = band[rows, :] + (real * grad_imag - imag * grad_real)
        return carry

    lax.fori_loop(0, (total + GROUP - 1) // GROUP, group, jnp.int32(0))

    col_copy.wait()
    out_copy.wait()
    real = band[:BAND, :] * scale
    imag = band[BAND:, :] * scale
    left = jnp.concatenate(
        [jnp.concatenate([real, imag], 1), jnp.concatenate([imag, -real], 1)], 0
    ).astype(jnp.bfloat16)
    mixed = dot(out_v[...].astype(jnp.bfloat16), left).astype(jnp.bfloat16)
    result[0] = lax.dot_general(
        mixed, col_v[...], (((1,), (1,)), ((), ())), preferred_element_type=jnp.float32
    )


def adjoint(own, other, infos, pupil, tables, col_table, out_table, n_tile):
    n_src = len(infos)
    portion = out_table.shape[1]
    columns = col_table.shape[0]
    places = n_src * SLOTS + GROUP
    return pl.pallas_call(
        functools.partial(adjoint_kernel, n_src, n_tile),
        out_shape=jax.ShapeDtypeStruct((1, portion, columns), jnp.float32),
        in_specs=[VMEM, VMEM] + [SMEM] * n_src + [VMEM] * 5 + [ANY, ANY],
        out_specs=VMEM,
        scratch_shapes=[
            pltpu.VMEM((2 * BAND, BAND), jnp.float32),
            pltpu.VMEM((2 * GRID, GRID), jnp.float32),
            pltpu.VMEM((2 * BAND, BAND), jnp.float32),
            pltpu.VMEM((columns, 2 * BAND), jnp.bfloat16),
            pltpu.VMEM(out_table.shape[1:], jnp.float32),
            pltpu.SMEM((places,), jnp.int32),
            pltpu.SMEM((places,), jnp.int32),
            pltpu.SMEM((places,), jnp.float32),
            pltpu.SemaphoreType.DMA((2,)),
        ],
        compiler_params=pltpu.CompilerParams(vmem_limit_bytes=32 * 1024 * 1024),
        cost_estimate=pl.CostEstimate(
            flops=2 * 128 * 4096 * 256, bytes_accessed=4 * 1024 * 1024, transcendentals=0
        ),
        name="adjoint",
    )(own, other, *infos, pupil, *tables, col_table, out_table)


def body(mask, cotangent, pupil_phase, source_weight, shift_table, source_ids, source_count):
    height, columns = mask.shape
    n_tile, n_src = lax.axis_size("tile"), lax.axis_size("src")
    col_table, row_table, out_table = image_tables(columns, height, n_tile, n_src)
    partial, pupil, slots = forward(
        source_ids,
        source_count,
        mask,
        cotangent,
        pupil_phase,
        source_weight.reshape(-1, 128),
        shift_table.T,
        col_table,
        row_table,
    )
    infos = [slots]
    for step in range(1, n_src):
        turn = [(place, (place + step) % n_src) for place in range(n_src)]
        infos.append(lax.ppermute(slots, "src", turn))
    other = jnp.zeros_like(partial)
    if n_tile & (n_tile - 1):
        partial = lax.psum(partial, "tile")
    else:
        step = 1
        while step < n_tile:
            partial = partial + other if step > 1 else partial
            swap = [(place, place ^ step) for place in range(n_tile)]
            other = lax.ppermute(partial, "tile", swap)
            step *= 2
    return adjoint(
        partial, other, infos, pupil, grid_tables(), col_table, out_table, n_tile
    )


def solution(mesh):
    placed = (
        P(("grp", "tile"), None),
        P(("grp", "tile"), None),
        P(),
        P(),
        P(),
        P(("grp", "src"), None),
        P(("grp", "src")),
    )
    return jax.shard_map(
        body, mesh=mesh, in_specs=placed, out_specs=P(("grp", "tile"), "src", None), check_vma=False
    )
```

time: 525 us -> 34 us (0.06)
  local copies, waits for them, and re-layouts: 162 us -> 9.12 us
  matrix products: 135 us -> 0 us
  waiting for transfers between devices: 134 us -> 5.47 us
  loops' own time: 58.3 us -> 0 us
  other arithmetic: 17.2 us -> 0.02 us
  between operations: 13.2 us -> 0.74 us
  Pallas kernels: 0 us -> 10.5 us
  starting transfers between devices: 0.31 us -> 8.05 us
    dot_general x51 -> x0, matrix products: 135 us -> none  [the longest x32 73.4 us: contract_rows(): lax.dot_general(left, right, (((0,), (0,)), ((), ())), precision=lax.Prec...]
    reduce_scatter x1 -> x0, waiting for transfers between devices: 76.9 us -> none  [body(): lax.psum_scatter(lax.dot_general(mixed, back_cols, (((1,), (1,)), ((), ()...]
    another operation x1 -> x0, loops' own time: 58.3 us -> none  [body(): band_grad = lax.fori_loop(jnp.int32(0), source_count[0], own_slot, empty)]
    psum x2 -> x0, waiting for transfers between devices: 57.1 us -> none  [the longest x1 29.5 us: body(): tile_grad = lax.psum(band_grad, 'tile')]
    while x72 -> x0, local copies, waits for them, and re-layouts: 42.7 us -> none
    mul x8 -> x0, local copies, waits for them, and re-layouts: 37.9 us -> none  [contribution(): field.reshape(2, height, columns) * factor * cotangent[None]]
    dynamic_slice x40 -> x0, local copies, waits for them, and re-layouts: 34 us -> none  [the longest x8 11.4 us: contribution(): offset_x = shift_table[source, 0]]
    convert_element_type x8 -> x0, local copies, waits for them, and re-layouts: 33.4 us -> none  [contribution(): field.reshape(2, height, columns) * factor * cotangent[None]]
  transfers between devices with their start and end apart: 3 -> 5, of which waited for: 3 -> 4; matrix products, arithmetic and copies ran while one was open for 1% -> 0% of each run, Pallas kernels for 0% -> 0%
where the time goes in v1:
time: 34 us; the launch traced here: 33.9 us
  Pallas kernels  10.5 us (31%)
  local copies, waits for them, and re-layouts  9.12 us (27%)
  starting transfers between devices  8.05 us (24%)
  waiting for transfers between devices  5.47 us (16%)
  between operations  0.74 us (2%)
    unnamed x28, local copies, waits for them, and re-layouts  9.12 us
    pallas_call x1, Pallas kernels, adjoint(): pl.pallas_call(functools.partial(adjoint_kernel, n_src, n_tile), out_shap...  5.98 us
    ppermute x3, starting transfers between devices, body(): infos.append(lax.ppermute(slots, 'src', turn))  4.61 us
    pallas_call x1, Pallas kernels, forward(): pl.pallas_call(forward_kernel, out_shape=(jax.ShapeDtypeStruct((lines, BA...  4.53 us
    ppermute x3, waiting for transfers between devices, body(): infos.append(lax.ppermute(slots, 'src', turn))  4.39 us
    ppermute x2, starting transfers between devices, body(): other = lax.ppermute(partial, 'tile', swap)  3.45 us
    ppermute x2, waiting for transfers between devices, body(): other = lax.ppermute(partial, 'tile', swap)  1.07 us
  transfers between devices with their start and end apart: 5, of which 4 were waited for; matrix products, arithmetic and copies ran while one was open for 0% of the time, Pallas kernels for 0%

profile of v1, /device:TPU:0, one launch (start us, length us, event | category | flops | bytes accessed | tf_op | source)
XLA Modules:
  0.0 33.9 jit_solution(11625829959800998250)
XLA Ops:
  0.7 0.0 copy-start
  0.7 1.4 %copy-done = bf16[2048,384]{1,0:T(8,128)(2,1)S(1)} copy-done((bf16[2048,384]{1,0:T(8,128)(2,1)S(1)}, bf16[2048,384]{1,0:T(8,128)(2,1)}, u32[]{:S(2)}) %copy-start) | copy-done | bytes 1572888
  2.1 0.0 copy-start.3
  2.1 1.6 %copy-done.3 = bf16[512,2048]{1,0:T(8,128)(2,1)S(1)} copy-done((bf16[512,2048]{1,0:T(8,128)(2,1)S(1)}, bf16[512,2048]{1,0:T(8,128)(2,1)}, u32[]{:S(2)}) %copy-start.3) | copy-done | bytes 2097176
  3.7 0.0 copy-start.4
  3.7 1.6 %copy-done.4 = bf16[512,2048]{1,0:T(8,128)(2,1)S(1)} copy-done((bf16[512,2048]{1,0:T(8,128)(2,1)S(1)}, bf16[512,2048]{1,0:T(8,128)(2,1)}, u32[]{:S(2)}) %copy-start.4) | copy-done | bytes 2097176
  5.2 0.0 copy-start.5
  5.2 1.4 %copy-done.5 = bf16[4,384,512]{2,1,0:T(8,128)(2,1)S(1)} copy-done((bf16[4,384,512]{2,1,0:T(8,128)(2,1)S(1)}, bf16[4,384,512]{2,1,0:T(8,128)(2,1)}, u32[]{:S(2)}) %copy-start.5) | copy-done | bytes 1572888
  6.7 0.9 %copy-done.8 = s32[12288,2]{0,1:T(2,128)S(1)} copy-done((s32[12288,2]{0,1:T(2,128)S(1)}, s32[12288,2]{0,1:T(2,128)}, u32[]{:S(2)}) %copy-start.8) | copy-done | bytes 98328
  7.6 0.8 %copy-done.11 = f32[12288]{0:T(1024)S(1)} copy-done((f32[12288]{0:T(1024)S(1)}, f32[12288]{0:T(1024)}, u32[]{:S(2)}) %copy-start.11) | copy-done | bytes 49176
  8.3 0.8 %copy-done.12 = f32[64,64]{1,0:T(8,128)S(1)} copy-done((f32[64,64]{1,0:T(8,128)S(1)}, f32[64,64]{1,0:T(8,128)}, u32[]{:S(2)}) %copy-start.12) | copy-done | bytes 16408
  9.1 0.7 %copy-done.13 = s32[1,8]{1,0:T(1,128)S(1)} copy-done((s32[1,8]{1,0:T(1,128)S(1)}, s32[1,8]{1,0:T(1,128)}, u32[]{:S(2)}) %copy-start.13) | copy-done | bytes 56
  9.8 0.0 copy-start.9
  9.8 0.0 copy-start.10
  9.8 4.5 %forward.1 = (f32[384,128]{1,0:T(8,128)S(1)}, f32[128,128]{1,0:T(8,128)S(1)}, f32[8,128]{1,0:T(8,128)S(1)}) custom-call(s32[1,8]{1,0:T(1,128)S(1)} %copy-done.13, s32[1]{0:T(128)S(6)} %copy.15.count, bf16[512,2048]{1,0:T(8,128)(2,1)S(1)} %copy-done.3, bf16[512,2048]{1,0:T(8,128)(2,1)S(1)} %copy-done.4, f32[64,64]{1,0:T(8,128)S(1)} %copy-done.12, ...), custom_call_target="tpu_custom_call" | custom-call | flops 805306368 | bytes 6291456 | tf_op jit(solution)/shard_map/forward/pallas_call | solution.py:150
  14.3 0.5 %collective-permute-start = (f32[384,128]{1,0:T(8,128)S(1)}, f32[384,128]{1,0:T(8,128)S(1)}, u32[]{:S(2)}, u32[]{:S(2)}) collective-permute-start(f32[384,128]{1,0:T(8,128)S(1)} %get-tuple-element.8), channel_id=1, source_target_pairs={{0,1},{1,0},{2,3},{3,2},{4,5},{5,4},{6,7},{7,6},{8,9},{9,8},{10,11... | collective-permute-start | bytes 589832 | tf_op jit(solution)/shard_map/ppermute | solution.py:341
  14.9 1.1 %collective-permute-done = f32[384,128]{1,0:T(8,128)S(1)} collective-permute-done((f32[384,128]{1,0:T(8,128)S(1)}, f32[384,128]{1,0:T(8,128)S(1)}, u32[]{:S(2)}, u32[]{:S(2)}) %collective-permute-start) | collective-permute-done | bytes 196640 | tf_op jit(solution)/shard_map/ppermute | solution.py:341
  16.0 2.9 %collective-permute-start.1 = (f32[384,128]{1,0:T(8,128)S(1)}, f32[384,128]{1,0:T(8,128)S(1)}, u32[]{:S(2)}, u32[]{:S(2)}) collective-permute-start(f32[384,128]{1,0:T(8,128)S(1)} %add.3.refs_0_), channel_id=1, source_target_pairs={{0,2},{1,3},{2,0},{3,1},{4,6},{5,7},{6,4},{7,5},{8,10},{9,11},{10,... | collective-permute-start | bytes 589832 | tf_op jit(solution)/shard_map/ppermute | solution.py:341
  18.9 3.6 %collective-permute-start.4 = (f32[8,128]{1,0:T(8,128)S(1)}, f32[8,128]{1,0:T(8,128)S(1)}, u32[]{:S(2)}, u32[]{:S(2)}) collective-permute-start(f32[8,128]{1,0:T(8,128)S(1)} %get-tuple-element.9.refs_2_), channel_id=1, source_target_pairs={{0,12},{4,0},{8,4},{12,8},{1,13},{5,1},{9,5},{13,9},{2,14},{6,2},{... | collective-permute-start | bytes 12296 | tf_op jit(solution)/shard_map/ppermute | solution.py:332
  22.5 0.0 collective-permute-start.3
  22.5 1.0 %collective-permute-start.2 = (f32[8,128]{1,0:T(8,128)S(1)}, f32[8,128]{1,0:T(8,128)S(1)}, u32[]{:S(2)}, u32[]{:S(2)}) collective-permute-start(f32[8,128]{1,0:T(8,128)S(1)} %get-tuple-element.9.refs_2_), channel_id=1, source_target_pairs={{0,4},{4,8},{8,12},{12,0},{1,5},{5,9},{9,13},{13,1},{2,6},{6,10},{... | collective-permute-start | bytes 12296 | tf_op jit(solution)/shard_map/ppermute | solution.py:332
  23.5 0.3 collective-permute-done.4.refs_5_
  23.8 3.2 %collective-permute-done.3.refs_4_ = f32[8,128]{1,0:T(8,128)S(1)} collective-permute-done((f32[8,128]{1,0:T(8,128)S(1)}, f32[8,128]{1,0:T(8,128)S(1)}, u32[]{:S(2)}, u32[]{:S(2)}) %collective-permute-start.3) | collective-permute-done | bytes 4128 | tf_op jit(solution)/shard_map/ppermute | solution.py:332
  27.0 0.9 %collective-permute-done.2.refs_3_ = f32[8,128]{1,0:T(8,128)S(1)} collective-permute-done((f32[8,128]{1,0:T(8,128)S(1)}, f32[8,128]{1,0:T(8,128)S(1)}, u32[]{:S(2)}, u32[]{:S(2)}) %collective-permute-start.2) | collective-permute-done | bytes 4128 | tf_op jit(solution)/shard_map/ppermute | solution.py:332
  27.9 0.0 collective-permute-done.1.refs_1_
  27.9 0.0 copy-done.1
  27.9 0.0 copy-done.2
  27.9 0.0 copy-done.6
  27.9 0.0 copy-done.7
  27.9 0.0 copy-done.9
  27.9 0.0 copy-done.10
  27.9 6.0 %adjoint.1 = f32[1,128,2048]{2,1,0:T(8,128)} custom-call(f32[384,128]{1,0:T(8,128)S(1)} %add.3.refs_0_, f32[384,128]{1,0:T(8,128)S(1)} %collective-permute-done.1.refs_1_, f32[8,128]{1,0:T(8,128)S(1)} %get-tuple-element.9.refs_2_, f32[8,128]{1,0:T(8,128)S(1)} %collective-permute-done.2.refs_3_, f32[8,128]{1,0:T(8,128)S(1)} %collective-permute-done.3.refs_4_, ...), custom_call_target="tpu_custom_call" | custom-call | flops 268435456 | bytes 4194304 | tf_op jit(solution)/shard_map/adjoint/pallas_call | solution.py:290
  (9 shorter events, 0.0 us)
Async XLA Ops:
  0.7 1.4 %copy-start = (bf16[2048,384]{1,0:T(8,128)(2,1)S(1)}, bf16[2048,384]{1,0:T(8,128)(2,1)}, u32[]{:S(2)}) copy-start(bf16[2048,384]{1,0:T(8,128)(2,1)} %constant.14.clone.col_table.refs_11_) | copy-start | bytes 4718596
  2.1 1.6 %copy-start.3 = (bf16[512,2048]{1,0:T(8,128)(2,1)S(1)}, bf16[512,2048]{1,0:T(8,128)(2,1)}, u32[]{:S(2)}) copy-start(bf16[512,2048]{1,0:T(8,128)(2,1)} %mask.1) | copy-start | bytes 6291460
  3.7 1.6 %copy-start.4 = (bf16[512,2048]{1,0:T(8,128)(2,1)S(1)}, bf16[512,2048]{1,0:T(8,128)(2,1)}, u32[]{:S(2)}) copy-start(bf16[512,2048]{1,0:T(8,128)(2,1)} %cotangent.1) | copy-start | bytes 6291460
  5.2 1.4 %copy-start.5 = (bf16[4,384,512]{2,1,0:T(8,128)(2,1)S(1)}, bf16[4,384,512]{2,1,0:T(8,128)(2,1)}, u32[]{:S(2)}) copy-start(bf16[4,384,512]{2,1,0:T(8,128)(2,1)} %constant.15.clone.row_table) | copy-start | bytes 4718596
  6.7 0.9 %copy-start.8 = (s32[12288,2]{0,1:T(2,128)S(1)}, s32[12288,2]{0,1:T(2,128)}, u32[]{:S(2)}) copy-start(s32[12288,2]{0,1:T(2,128)} %param.18) | copy-start | bytes 294916
  7.5 0.8 %copy-start.11 = (f32[12288]{0:T(1024)S(1)}, f32[12288]{0:T(1024)}, u32[]{:S(2)}) copy-start(f32[12288]{0:T(1024)} %param.17) | copy-start | bytes 147460
  8.3 0.8 %copy-start.12 = (f32[64,64]{1,0:T(8,128)S(1)}, f32[64,64]{1,0:T(8,128)}, u32[]{:S(2)}) copy-start(f32[64,64]{1,0:T(8,128)} %phase.1) | copy-start | bytes 49156
  9.1 0.7 %copy-start.13 = (s32[1,8]{1,0:T(1,128)S(1)}, s32[1,8]{1,0:T(1,128)}, u32[]{:S(2)}) copy-start(s32[1,8]{1,0:T(1,128)} %ids.1) | copy-start | bytes 100
  9.8 18.1 %copy-start.1 = (bf16[2048,384]{1,0:T(8,128)(2,1)S(1)}, bf16[2048,384]{1,0:T(8,128)(2,1)}, u32[]{:S(2)}) copy-start(bf16[2048,384]{1,0:T(8,128)(2,1)} %constant.14.clone.col_table.refs_11_) | copy-start | bytes 4718596
  9.8 18.1 %copy-start.2 = (f32[16,128,256]{2,1,0:T(8,128)S(1)}, f32[16,128,256]{2,1,0:T(8,128)}, u32[]{:S(2)}) copy-start(f32[16,128,256]{2,1,0:T(8,128)} %constant.20.clone.refs_12_) | copy-start | bytes 6291460
  9.8 18.1 %copy-start.6 = (bf16[256,256]{1,0:T(8,128)(2,1)S(1)}, bf16[256,256]{1,0:T(8,128)(2,1)}, u32[]{:S(2)}) copy-start(bf16[256,256]{1,0:T(8,128)(2,1)} %constant.19.clone.refs_10_) | copy-start | bytes 393220
  9.8 18.1 %copy-start.7 = (bf16[256,256]{1,0:T(8,128)(2,1)S(1)}, bf16[256,256]{1,0:T(8,128)(2,1)}, u32[]{:S(2)}) copy-start(bf16[256,256]{1,0:T(8,128)(2,1)} %constant.16.clone.refs_7_) | copy-start | bytes 393220
  9.8 18.1 %copy-start.9 = (bf16[128,256]{1,0:T(8,128)(2,1)S(1)}, bf16[128,256]{1,0:T(8,128)(2,1)}, u32[]{:S(2)}) copy-start(bf16[128,256]{1,0:T(8,128)(2,1)} %constant.18.clone.refs_9_) | copy-start | bytes 196612
  9.8 18.1 %copy-start.10 = (bf16[256,128]{1,0:T(8,128)(2,1)S(1)}, bf16[256,128]{1,0:T(8,128)(2,1)}, u32[]{:S(2)}) copy-start(bf16[256,128]{1,0:T(8,128)(2,1)} %constant.17.clone.refs_8_) | copy-start | bytes 196612
  14.3 1.6 %collective-permute-start = (f32[384,128]{1,0:T(8,128)S(1)}, f32[384,128]{1,0:T(8,128)S(1)}, u32[]{:S(2)}, u32[]{:S(2)}) collective-permute-start(f32[384,128]{1,0:T(8,128)S(1)} %get-tuple-element.8), channel_id=1, source_target_pairs={{0,1},{1,0},{2,3},{3,2},{4,5},{5,4},{6,7},{7,6},{8,9},{9,8},{10,11... | collective-permute-start | bytes 589832 | tf_op jit(solution)/shard_map/ppermute | solution.py:341
  16.0 11.9 %collective-permute-start.1 = (f32[384,128]{1,0:T(8,128)S(1)}, f32[384,128]{1,0:T(8,128)S(1)}, u32[]{:S(2)}, u32[]{:S(2)}) collective-permute-start(f32[384,128]{1,0:T(8,128)S(1)} %add.3.refs_0_), channel_id=1, source_target_pairs={{0,2},{1,3},{2,0},{3,1},{4,6},{5,7},{6,4},{7,5},{8,10},{9,11},{10,... | collective-permute-start | bytes 589832 | tf_op jit(solution)/shard_map/ppermute | solution.py:341
  18.9 4.9 %collective-permute-start.4 = (f32[8,128]{1,0:T(8,128)S(1)}, f32[8,128]{1,0:T(8,128)S(1)}, u32[]{:S(2)}, u32[]{:S(2)}) collective-permute-start(f32[8,128]{1,0:T(8,128)S(1)} %get-tuple-element.9.refs_2_), channel_id=1, source_target_pairs={{0,12},{4,0},{8,4},{12,8},{1,13},{5,1},{9,5},{13,9},{2,14},{6,2},{... | collective-permute-start | bytes 12296 | tf_op jit(solution)/shard_map/ppermute | solution.py:332
  22.5 4.5 %collective-permute-start.3 = (f32[8,128]{1,0:T(8,128)S(1)}, f32[8,128]{1,0:T(8,128)S(1)}, u32[]{:S(2)}, u32[]{:S(2)}) collective-permute-start(f32[8,128]{1,0:T(8,128)S(1)} %get-tuple-element.9.refs_2_), channel_id=1, source_target_pairs={{0,8},{4,12},{8,0},{12,4},{1,9},{5,13},{9,1},{13,5},{2,10},{6,14},... | collective-permute-start | bytes 12296 | tf_op jit(solution)/shard_map/ppermute | solution.py:332
  22.5 5.4 %collective-permute-start.2 = (f32[8,128]{1,0:T(8,128)S(1)}, f32[8,128]{1,0:T(8,128)S(1)}, u32[]{:S(2)}, u32[]{:S(2)}) collective-permute-start(f32[8,128]{1,0:T(8,128)S(1)} %get-tuple-element.9.refs_2_), channel_id=1, source_target_pairs={{0,4},{4,8},{8,12},{12,0},{1,5},{5,9},{9,13},{13,1},{2,6},{6,10},{... | collective-permute-start | bytes 12296 | tf_op jit(solution)/shard_map/ppermute | solution.py:332
